TPU v7x, 256 devices: a whole 4x4x8 slice. The times are simulated.
256 devices in a mesh: expert: 64 (over y, z, core), tensor: 4 (over x).
Axes of the slice: x: 4, y: 4, z: 8, core: 2. Of those that a mesh axis runs over, the one named last changes fastest.
Arguments:
- hidden: bfloat16 [1024, 4096], P('expert'), may hold values from -90 to 90
- norm_gain: float32 [4, 4096], replicated, may hold values from 0.5 to 1.5
- head_weight: bfloat16 [4096, 4, 64128], P(None, 'tensor', 'expert'), may hold values from -8 to 8
- expert_ids: int32 [1024, 2], P('expert'), may hold values from 0 to 3, as said below
- mix_weight: int32 [1024, 2], P('expert'), may hold values from 1 to 65535
Outputs:
- mixed_logprob: float32 [1024, 64128], P('expert', 'tensor')
Inputs may be any that keep to these rules, and one draw needn't show every extreme that they name: `expert_ids`: each row names 2 different experts. Among the 16 rows of each index of expert, one expert, the same for every index and drawn from the seed, is named by exactly 15 rows, and no expert by more than 15 rows.
All inputs are finite; a program needn't handle non-finite values.
Results may differ from a plain program's by a relative error of at most 0.00063.
Values may be sent and summed in bfloat16 or wider, within the bound.
A program may use at most 128 MiB of HBM per device.

v0:
```python
import jax
import jax.numpy as jnp
from jax import lax
from jax.sharding import PartitionSpec as P

EXPERTS = 4


EPS = 1e-05
FAR = -1e30


def routing_ranks(expert_ids):
    onehot = (expert_ids[:, :, None] == jnp.arange(EXPERTS, dtype=jnp.int32)[None, None, :]).astype(
        jnp.int32
    )
    member = jnp.sum(onehot, axis=1)
    earlier = jnp.cumsum(member, axis=0) - member
    return jnp.sum(onehot * earlier[:, None, :], axis=2)


def per_device(hidden, norm_gain, head_weight, expert_ids, mix_weight):
    n_expert = lax.axis_size("expert")
    group_size = n_expert // EXPERTS
    rows_dev = hidden.shape[0]
    features = hidden.shape[1]
    per_source = rows_dev - 1
    capacity = n_expert * per_source
    own_expert = lax.axis_index("expert") // group_size
    ranks = routing_ranks(expert_ids)
    all_rows, all_codes = (
        lax.all_gather(hidden, "expert", axis=0, tiled=True),
        lax.all_gather(expert_ids.astype(jnp.bfloat16), "expert", axis=0, tiled=True),
    )
    codes = all_codes.astype(jnp.int32)
    chosen = jnp.sum((codes == own_expert).astype(jnp.int32), axis=1).reshape(n_expert, rows_dev)
    placed = jnp.cumsum(chosen, axis=1) - chosen
    slot_index = jnp.arange(n_expert, dtype=jnp.int32)[:, None] * per_source + placed
    target = jnp.where(chosen == 1, slot_index, capacity).reshape(-1)
    source_row = (
        jnp.zeros((capacity + 1,), jnp.int32)
        .at[target]
        .set(jnp.arange(n_expert * rows_dev, dtype=jnp.int32))
    )
    slot_rows = all_rows[source_row[:capacity]]
    hidden_f32 = slot_rows.astype(jnp.float32)
    rms_scale = jnp.sqrt(jnp.mean(hidden_f32 * hidden_f32, axis=1, keepdims=True) + EPS)
    gain_row = lax.dynamic_index_in_dim(norm_gain, own_expert, 0, keepdims=False)
    normed = (hidden_f32 / rms_scale * gain_row).astype(jnp.bfloat16)
    local_head = head_weight.reshape(features, head_weight.shape[2])
    logits = jnp.dot(normed, local_head, preferred_element_type=jnp.float32)
    row_top = jnp.max(logits, axis=1)
    owned = (jnp.arange(EXPERTS, dtype=jnp.int32) == own_expert)[:, None]
    top_all = lax.pmax(jnp.where(owned, row_top[None, :], FAR), ("expert", "tensor"))
    global_top = lax.dynamic_index_in_dim(top_all, own_expert, 0, keepdims=False)
    raised = jnp.exp(logits - global_top[:, None])
    sum_all = lax.psum(
        jnp.where(owned, jnp.sum(raised, axis=1)[None, :], 0.0), ("expert", "tensor")
    )
    row_total = lax.dynamic_index_in_dim(sum_all, own_expert, 0, keepdims=False)
    probs = (raised / row_total[:, None]).astype(jnp.bfloat16)
    returned = lax.all_to_all(probs, "expert", split_axis=0, concat_axis=1, tiled=True)
    returned = returned.reshape(per_source, EXPERTS, -1)
    counts = mix_weight.astype(jnp.float32)
    shares = counts / jnp.sum(counts, axis=1, keepdims=True)
    mixture = jnp.zeros((rows_dev, returned.shape[2]), jnp.float32)
    for slot_k in range(expert_ids.shape[1]):
        picked = returned[ranks[:, slot_k], expert_ids[:, slot_k]]
        mixture = mixture + shares[:, slot_k : slot_k + 1] * picked.astype(jnp.float32)
    return jnp.log(mixture)


def solution(mesh):
    placed = (
        P("expert", None),
        P(),
        P(None, "tensor", "expert"),
        P("expert", None),
        P("expert", None),
    )
    return jax.shard_map(
        per_device, mesh=mesh, in_specs=placed, out_specs=P("expert", "tensor"), check_vma=False
    )
```

profile of v0, /device:TPU:1, one launch (start us, length us, event | category | flops | bytes accessed | tf_op | source)
XLA Modules:
  0.0 369.7 jit_solution(12777108559282120249)
XLA Ops:
  6.5 0.0 copy-start
  6.5 0.0 all-gather.3.cloned.1.call-start
  6.5 0.7 all-gather.3.cloned.1.call-update
  7.3 0.7 convert_bitcast_fusion
  8.0 44.2 %all-gather = bf16[64,16,2]{1,2,0:T(2,128)(2,1)S(1)} all-gather(bf16[1,16,2]{1,2,0:T(2,128)(2,1)S(1)} %convert_bitcast_fusion), channel_id=1, replica_groups=mesh['expert'=64,'tensor'=4] {'expert'}, dimensions={0}, use_global_device_ids=true | all-gather | bytes 4160 | tf_op jit(solution)/shard_map/all_gather | solution.py:33
  52.2 0.1 copy.21
  52.3 0.1 copy.23
  52.3 0.2 reduce_window_sum.24
  52.5 0.1 reshape.132
  52.6 0.1 copy.22
  52.7 0.1 reshape.131
  52.8 0.1 add.77
  52.9 0.1 add.78
  53.0 4.3 %scatter_custom_fusion = s32[961]{0:T(1024)S(1)} fusion(s32[1024]{0:T(1024)S(1)} %bitcast.25, s32[1024]{0:T(1024)S(1)} %iota.18, s32[]{:T(128)} %constant.26.clone.1), kind=kCustom, calls=%fused_computation.32 | custom fusion | bytes 3848 | tf_op jit(solution)/shard_map/scatter | solution.py:43
  57.4 0.0 copy-done
  57.4 40.1 %all-gather.3.cloned.1.call-done = bf16[1024,4096]{1,0:T(8,128)(2,1)} async-done(((bf16[16,4096]{1,0:T(8,128)(2,1)}), bf16[1024,4096]{1,0:T(8,128)(2,1)}) %all-gather.3.cloned.1.call-update) | async-done | bytes 8388624 | tf_op jit(solution)/shard_map/all_gather | solution.py:32
  97.6 19.4 %gather_fusion = bf16[960,4096]{1,0:T(8,128)(2,1)} fusion(bf16[1024,4096]{1,0:T(8,128)(2,1)} %all-gather.3.cloned.1.call-done, s32[1024]{0:T(1024)S(1)} %pad_clamp_fusion), kind=kCustom, calls=%fused_computation | custom fusion | bytes 15732480 | tf_op jit(solution)/shard_map/gather | solution.py:45
  116.9 0.0 copy-start.1
  116.9 5.0 %fusion = f32[960]{0:T(1024)S(1)} fusion(bf16[960,4096]{1,0:T(8,128)(2,1)} %gather_fusion), kind=kLoop, calls=%fused_computation.6 | loop fusion | flops 11795520 | bytes 7868160 | tf_op jit(solution)/shard_map/reduce_sum | solution.py:47
  121.9 0.5 copy-done.1
  122.4 12.2 %fusion.22 = (f32[960]{0:T(1024)S(1)}, f32[960,1002]{1,0:T(8,128)}) fusion(bf16[4096,1,1002]{0,2,1:T(8,128)(2,1)} %param.7, bf16[960,4096]{1,0:T(8,128)(2,1)S(1)} %copy-done.1, f32[4096]{0:T(1024)S(1)} %bitcast.23, f32[960]{0:T(1024)S(1)} %add_sqrt_fusion), kind=kOutput, calls=%fused_computation.56 | convolution fusion | flops 7896738304 | bytes 19944448 | tf_op jit(solution)/shard_map/dot_general | solution.py:51
  134.6 0.1 broadcast_select_fusion.1
  134.6 75.2 %pmax.7 = f32[4,960]{1,0:T(4,128)S(1)} all-reduce(f32[4,960]{1,0:T(4,128)S(1)} %broadcast_select_fusion.1), channel_id=1, replica_groups=mesh['expert'=64,'tensor'=4] {'expert','tensor'}, use_global_device_ids=true, to_apply=%region_6.7 | all-reduce | flops 3840 | bytes 30720 | tf_op jit(solution)/shard_map/pmax | solution.py:54
  209.8 3.0 fusion.7
  212.8 0.0 copy-start.2
  212.8 0.0 copy-start.3
  212.9 0.1 broadcast_select_fusion
  212.9 73.4 %psum.7 = f32[4,960]{1,0:T(4,128)S(1)} all-reduce(f32[4,960]{1,0:T(4,128)S(1)} %broadcast_select_fusion), channel_id=1, replica_groups=mesh['expert'=64,'tensor'=4] {'expert','tensor'}, use_global_device_ids=true, to_apply=%region_8.9 | all-reduce | flops 3840 | bytes 30720 | tf_op jit(solution)/shard_map/psum | solution.py:57
  286.4 2.8 divide_convert_fusion
  289.2 1.8 all_to_all.12
  290.9 8.4 %all-to-all-start = ((bf16[64,15,1002]{2,1,0:T(8,128)(2,1)}), bf16[64,15,1002]{2,1,0:T(8,128)(2,1)S(1)}, u32[]{:S(2)}, u32[]{:S(2)}) async-start(bf16[64,15,1002]{2,1,0:T(8,128)(2,1)} %all_to_all.12), calls=%async_computation | async-start | bytes 4194304 | tf_op jit(solution)/shard_map/all_to_all | solution.py:62
  299.4 0.0 copy-done.2
  299.4 0.1 copy.26
  299.5 0.1 copy.28
  299.6 0.0 copy-done.3
  299.7 50.9 %all-to-all-done = bf16[64,15,1002]{2,1,0:T(8,128)(2,1)S(1)} async-done(((bf16[64,15,1002]{2,1,0:T(8,128)(2,1)}), bf16[64,15,1002]{2,1,0:T(8,128)(2,1)S(1)}, u32[]{:S(2)}, u32[]{:S(2)}) %all-to-all-start) | async-done | bytes 1923872 | tf_op jit(solution)/shard_map/all_to_all | solution.py:62
  350.6 2.4 copy.25
  353.0 4.4 %reshape.91 = bf16[15,4,16032]{2,1,0:T(4,128)(2,1)S(1)} reshape(bf16[15,64,1002]{2,1,0:T(8,128)(2,1)} %copy.25) | data formatting | bytes 3847680 | tf_op jit(solution)/shard_map/reshape | solution.py:63
  357.5 2.1 gather_fusion.1
  359.5 2.1 gather_fusion.2
  361.6 1.3 add_log_fusion
  (21 shorter events, 0.2 us)
Async XLA Ops:
  6.5 50.9 %copy-start = (f32[4,4096]{1,0:T(4,128)S(1)}, f32[4,4096]{1,0:T(4,128)}, u32[]{:S(2)}) copy-start(f32[4,4096]{1,0:T(4,128)} %param.6) | copy-start | bytes 196612
  6.5 91.0 %all-gather.3.cloned.1.call-start = ((), (), s32[]{:S(2)}) async-start(), calls=%async_computation.1 | async-start | bytes 8519680 | tf_op jit(solution)/shard_map/all_gather | solution.py:32
  116.9 5.5 %copy-start.1 = (bf16[960,4096]{1,0:T(8,128)(2,1)S(1)}, bf16[960,4096]{1,0:T(8,128)(2,1)}, u32[]{:S(2)}) copy-start(bf16[960,4096]{1,0:T(8,128)(2,1)} %gather_fusion) | copy-start | bytes 23592964
  212.8 86.5 %copy-start.2 = (s32[16,2]{0,1:T(2,128)S(1)}, s32[16,2]{0,1:T(2,128)}, u32[]{:S(2)}) copy-start(s32[16,2]{0,1:T(2,128)} %param.8) | copy-start | bytes 388
  212.8 86.7 %copy-start.3 = (s32[16,2]{0,1:T(2,128)S(1)}, s32[16,2]{0,1:T(2,128)}, u32[]{:S(2)}) copy-start(s32[16,2]{0,1:T(2,128)} %param.9) | copy-start | bytes 388
  290.9 59.7 %all-to-all-start = ((bf16[64,15,1002]{2,1,0:T(8,128)(2,1)}), bf16[64,15,1002]{2,1,0:T(8,128)(2,1)S(1)}, u32[]{:S(2)}, u32[]{:S(2)}) async-start(bf16[64,15,1002]{2,1,0:T(8,128)(2,1)} %all_to_all.12), calls=%async_computation | async-start | bytes 4194304 | tf_op jit(solution)/shard_map/all_to_all | solution.py:62
Sparse Core Ops, SparseCore 0:
  10.1 87.3 all-gather.2
where the time goes:
time: 370 us
  blocking collectives  193 us (52%)
  waiting for transfers between devices  91.7 us (25%)
  local copies, waits for them, and re-layouts  37.7 us (10%)
  between operations  13.6 us (4%)
  other arithmetic  13.3 us (4%)
  matrix products  12.2 us (3%)
  starting transfers between devices  8.43 us (2%)
    pmax x1, blocking collectives, per_device(): lax.pmax(jnp.where(owned, row_top[None, :], FAR), ('expert', 'tensor'))  75.2 us
    psum x1, blocking collectives, per_device(): lax.psum(jnp.where(owned, jnp.sum(raised, axis=1)[None, :], 0.0), ('exper...  73.4 us
    all_to_all x1, waiting for transfers between devices, per_device(): lax.all_to_all(probs, 'expert', split_axis=0, concat_axis=1, tiled=True)  50.9 us
    all_gather x1, blocking collectives, per_device(): lax.all_gather(expert_ids.astype(jnp.bfloat16), 'expert', axis=0, tiled=T...  44.2 us
    all_gather x1, waiting for transfers between devices, per_device(): lax.all_gather(hidden, 'expert', axis=0, tiled=True)  40.1 us
    gather x1, local copies, waits for them, and re-layouts, per_device(): slot_rows = all_rows[source_row[:capacity]]  19.4 us
    dot_general x1, matrix products, per_device(): logits = jnp.dot(normed, local_head, preferred_element_type=jnp.float32)  12.2 us
    all_to_all x1, starting transfers between devices, per_device(): lax.all_to_all(probs, 'expert', split_axis=0, concat_axis=1, tiled=True)  8.43 us
  transfers between devices with their start and end apart: 2, of which 2 were waited for; matrix products, arithmetic and copies ran while one was open for 2% of the time, Pallas kernels for 0%

commit v1 on v0

v1 whole, which is shorter than its diff:
```python
import jax
import jax.numpy as jnp
from jax import lax
from jax.experimental import pallas as pl
from jax.experimental.pallas import tpu as pltpu
from jax.sharding import PartitionSpec as P

EPS = 1e-05
FAR = -1e30
NX, NY, NZ, NC = 4, 4, 8, 2
ROWS_DEV = 16
D = 4096
FQ = D // NX
VD = 1002
VP = 1024
FA = 640
FB = FQ - FA
MESH = pl.DeviceIdType.MESH
F32 = jnp.float32
BF16 = jnp.bfloat16

SLOT = {0: 0, 7: 1, 1: 2, 6: 3, 2: 4, 5: 5, 3: 6, 4: 7}
DZ = {s: d for d, s in SLOT.items()}


def sem_table():
    names = []
    names += [("y", k) for k in range(1, NY)]
    names += [("sy", k) for k in range(1, NY)]
    names += [("sz", dz, dc) for dz in range(NZ) for dc in range(NC) if (dz, dc) != (0, 0)]
    names += [("az", dz) for dz in range(1, NZ)]
    names += [("ax", dz, dx) for dz in range(NZ) for dx in range(1, NX)]
    names += [("bx", dx) for dx in range(1, NX)]
    names += [("bz", dz, dx) for dz in range(1, NZ) for dx in range(NX)]
    names += [("cc", dz, dx) for dz in range(NZ) for dx in range(NX)]
    names += [("tx", dx, dc) for dx in range(NX) for dc in range(NC) if (dx, dc) != (0, 0)]
    names += [("tz", dz) for dz in range(1, NZ)]
    names += [(kind, sign, q) for kind in ("far", "near", "sum") for sign in (1, -1) for q in range(2)]
    names += [("rz", dz, dc) for dz in range(NZ) for dc in range(NC) if (dz, dc) != (0, 0)]
    return {name: i for i, name in enumerate(names)}


SEMS = sem_table()


def body(h_ref, g_ref, ids_ref, mw_ref, w_ref, out_ref,
         wt, n4, gat, sh_src, sh_y, sh_all, lg, mcol, st_own, st_x, st_zsrc, st_z,
         fm, fs, cm, cf, pr, far_in, near_in, sum_in, mix, w_sem, loc_sem, ss, rs):
    me = lax.axis_index("expert")
    x = lax.axis_index("tensor")
    y = me // (NZ * NC)
    z = (me // NC) % NZ
    c = me % NC

    def dev(dx=0, dy=0, dz=0, dc=0):
        yy = (y + dy) % NY
        zz = (z + dz) % NZ
        cc = (c + dc) % NC
        return ((yy * NZ + zz) * NC + cc, (x + dx) % NX)

    sent = []

    def send(key, src, dst, to):
        k = SEMS[key]
        copy = pltpu.make_async_remote_copy(
            src_ref=src, dst_ref=dst, send_sem=ss.at[k], recv_sem=rs.at[k],
            device_id=to, device_id_type=MESH)
        copy.start()
        sent.append(copy)

    def arrive(key, dst):
        k = SEMS[key]
        pltpu.make_async_remote_copy(
            src_ref=dst, dst_ref=dst, send_sem=ss.at[k], recv_sem=rs.at[k],
            device_id=dev(dc=1), device_id_type=MESH).wait_recv()

    w_copy = pltpu.make_async_copy(w_ref, wt, w_sem)
    w_copy.start()

    peers = [dev(dy=k) for k in range(1, NY)]
    peers += [dev(dz=a, dc=b) for a in range(NZ) for b in range(NC) if (a, b) != (0, 0)]
    peers += [dev(dx=a, dc=b) for a in range(1, NX) for b in range(NC)]
    barrier = pltpu.get_barrier_semaphore()
    for peer in peers:
        pl.semaphore_signal(barrier, inc=1, device_id=peer, device_id_type=MESH)

    h_all = h_ref[...].astype(F32)
    rms = jnp.sqrt(jnp.mean(h_all * h_all, axis=1, keepdims=True) + EPS)
    cols = pl.ds(pl.multiple_of(x * FQ, FQ), FQ)
    h_q = h_ref[:, cols].astype(F32) / rms
    for e in range(NY):
        n4[e] = (h_q * g_ref[pl.ds(e, 1), cols]).astype(BF16)
    counts = mw_ref[...].astype(F32)
    shares = counts / (counts[:, 0:1] + counts[:, 1:2])
    ids = ids_ref[...]
    lane = lax.broadcasted_iota(jnp.int32, (ROWS_DEV, 128), 1)
    row = lax.broadcasted_iota(jnp.int32, (ROWS_DEV, 128), 0)
    mine = lane - row == c * 64 + y * ROWS_DEV
    for e in range(NY):
        col = jnp.sum(jnp.where(ids == e, shares, 0.0), axis=1, keepdims=True)
        line = jnp.sum(jnp.where(mine, col, 0.0), axis=0, keepdims=True)
        sh_src[e] = jnp.broadcast_to(line, (8, 128))

    pl.semaphore_wait(barrier, len(peers))

    for k in (2, 1, 3):
        send(("y", k), n4.at[(y + k) % NY], gat.at[0, x, c, y], dev(dy=k))
    for k in (2, 1, 3):
        send(("sy", k), sh_src.at[(y + k) % NY], sh_y.at[k], dev(dy=k))
    own = pltpu.make_async_copy(n4.at[y], gat.at[0, x, c, y], loc_sem)
    own.start()
    own.wait()
    for k in (1, 3, 2):
        arrive(("y", k), gat.at[0, x, c, (y - k) % NY])

    def unit(dz, dx):
        return gat.at[SLOT[dz], (x + dx) % NX, c]

    def part_a(dz, dx):
        return gat.at[SLOT[dz], (x + dx) % NX, c, :, :, pl.ds(0, FA)]

    def part_b(dz, dx):
        return gat.at[SLOT[dz], (x + dx) % NX, c, :, :, pl.ds(FA, FB)]

    def a_along_z(dz, step):
        to = (dz - step) % NZ
        send(("az", to), part_a(dz, 0), part_a(to, 0), dev(dz=step))

    def a_along_x(dz):
        send(("ax", dz, 3), part_a(dz, 0), part_a(dz, 0), dev(dx=1))
        send(("ax", dz, 1), part_a(dz, 0), part_a(dz, 0), dev(dx=-1))

    def a_opposite(dz):
        for dx in (3, 1):
            arrive(("ax", dz, dx), part_a(dz, dx))
            if dx == (3 if dz % 2 == 0 else 1):
                step = 1 if dx == 3 else -1
                send(("ax", dz, 2), part_a(dz, dx), part_a(dz, dx), dev(dx=step))

    def b_along_z(dz, dx, step):
        to = (dz - step) % NZ
        send(("bz", to, dx), part_b(dz, dx), part_b(to, dx), dev(dz=step))

    def to_sibling(dz, dx):
        send(("cc", dz, dx), unit(dz, dx), unit(dz, dx), dev(dc=1))

    def right_hops(dx):
        return 4 if dx in (0, 1) else 3

    def b_round(k, dx):
        if k <= right_hops(dx):
            arrive(("bz", NZ - k, dx), part_b(NZ - k, dx))
            if k < right_hops(dx):
                b_along_z(NZ - k, dx, 1)
        if k <= 7 - right_hops(dx):
            arrive(("bz", k, dx), part_b(k, dx))
            if k < 7 - right_hops(dx):
                b_along_z(k, dx, -1)

    def logits(g):
        rows = 2 * 128

        def tile(n, carry):
            vocab = pl.ds(pl.multiple_of(n * 256, 256), 256)
            acc = jnp.zeros((rows, 256), F32)
            for xi in range(NX):
                lhs = gat[2 * g:2 * g + 2, xi].reshape(rows, FQ)
                acc += lax.dot_general(
                    lhs, wt[vocab, xi * FQ:(xi + 1) * FQ],
                    (((1,), (1,)), ((), ())), preferred_element_type=F32)
            lg[g * rows:(g + 1) * rows, vocab] = acc
            return carry

        lax.fori_loop(0, 3, tile, 0)
        acc = jnp.zeros((rows, VD - 768), F32)
        for xi in range(NX):
            lhs = gat[2 * g:2 * g + 2, xi].reshape(rows, FQ)
            acc += lax.dot_general(
                lhs, wt[768:VD, xi * FQ:(xi + 1) * FQ],
                (((1,), (1,)), ((), ())), preferred_element_type=F32)
        lg[g * rows:(g + 1) * rows, 768:VP] = jnp.concatenate(
            [acc, jnp.full((rows, VP - VD), FAR, F32)], axis=1)

        def stat(i, carry):
            at = pl.ds(pl.multiple_of(g * rows + i * 32, 32), 32)
            block = lg[at, :]
            top = jnp.max(block, axis=1, keepdims=True)
            total = jnp.sum(jnp.exp(block - top), axis=1, keepdims=True)
            mcol[0, at, :] = jnp.broadcast_to(top, (32, 128))
            mcol[1, at, :] = jnp.broadcast_to(total, (32, 128))
            return carry

        lax.fori_loop(0, rows // 32, stat, 0)
        for s in (2 * g, 2 * g + 1):
            at = (z + DZ[s]) % NZ
            for j in range(2):
                st_own[pl.ds(j * 8 + at, 1), :] = jnp.sum(
                    jnp.where(eye(), mcol[j, s * 128:(s + 1) * 128, :], 0.0), axis=0, keepdims=True)

    def eye():
        return (lax.broadcasted_iota(jnp.int32, (128, 128), 0)
                == lax.broadcasted_iota(jnp.int32, (128, 128), 1))

    a_along_z(0, 1)
    a_along_z(0, -1)
    send(("bx", 3), part_b(0, 0), part_b(0, 0), dev(dx=1))
    send(("bx", 1), part_b(0, 0), part_b(0, 0), dev(dx=-1))
    a_along_x(0)
    b_along_z(0, 0, 1)
    b_along_z(0, 0, -1)
    to_sibling(0, 0)

    for k in (1, 3, 2):
        arrive(("sy", k), sh_y.at[k])
    sh_all[0, c] = sh_src[y] + sh_y[1] + sh_y[2] + sh_y[3]
    for dz in range(NZ):
        for dc in range(NC):
            if (dz, dc) != (0, 0):
                send(("sz", (-dz) % NZ, dc), sh_all.at[0, c], sh_all.at[(-dz) % NZ, c],
                     dev(dz=dz, dc=dc))

    for dx in (3, 1, 2):
        arrive(("bx", dx), part_b(0, dx))
        if dx == 3:
            send(("bx", 2), part_b(0, 3), part_b(0, 3), dev(dx=1))
        b_along_z(0, dx, 1)
        b_along_z(0, dx, -1)

    def finish_x(dz):
        for dx in range(1, NX):
            if dx == 2:
                arrive(("ax", dz, 2), part_a(dz, 2))
            to_sibling(dz, dx)

    def from_sibling(dz):
        for dx in range(NX):
            arrive(("cc", dz, dx), gat.at[SLOT[dz], (x + dx) % NX, 1 - c])

    for k in range(1, 5):
        arrive(("az", NZ - k), part_a(NZ - k, 0))
        if k < 4:
            a_along_z(NZ - k, 1)
        a_along_x(NZ - k)
        if k < 4:
            arrive(("az", k), part_a(k, 0))
            if k < 3:
                a_along_z(k, -1)
            a_along_x(k)
        if k == 1:
            a_opposite(0)
        else:
            a_opposite(NZ - k + 1)
            a_opposite(k - 1)
        for dx in range(NX):
            b_round(k, dx)
        if k < 4:
            to_sibling(NZ - k, 0)
            to_sibling(k, 0)
        else:
            to_sibling(4, 0)
        if k == 1:
            finish_x(0)
            w_copy.wait()
        else:
            finish_x(NZ - k + 1)
            finish_x(k - 1)
        if k == 2:
            from_sibling(0)
            from_sibling(7)
            logits(0)
        if k == 3:
            from_sibling(1)
            from_sibling(6)
            logits(1)
    a_opposite(4)
    finish_x(4)
    from_sibling(2)
    from_sibling(5)
    logits(2)
    from_sibling(3)
    from_sibling(4)
    logits(3)

    def merge(parts):
        top = parts[0][0]
        for m, _ in parts[1:]:
            top = jnp.maximum(top, m)
        total = jnp.zeros_like(top)
        for m, s in parts:
            total += s * jnp.exp(m - top)
        return top, total

    near_peers = [(a, b) for a in range(NX) for b in range(NC) if (a, b) != (0, 0)]
    for a, b in near_peers:
        send(("tx", (-a) % NX, b), st_own, st_x.at[(-a) % NX, b], dev(dx=a, dc=b))
    parts = [(st_own[0:8], st_own[8:16])]
    for a, b in near_peers:
        arrive(("tx", a, b), st_x.at[a, b])
        parts.append((st_x[a, b, 0:8], st_x[a, b, 8:16]))
    top, total = merge(parts)
    st_zsrc[0:8] = top
    st_zsrc[8:16] = total
    for k in range(1, NZ):
        send(("tz", (-k) % NZ), st_zsrc, st_z.at[(-k) % NZ], dev(dz=k))
    for dz in range(NZ):
        for dc in range(NC):
            if (dz, dc) != (0, 0):
                arrive(("sz", dz, dc), sh_all.at[dz, (c + dc) % NC])
    parts = [(top, total)]
    for k in range(1, NZ):
        arrive(("tz", k), st_z.at[k])
        parts.append((st_z[k, 0:8], st_z[k, 8:16]))
    top, total = merge(parts)
    fm[...] = top
    fs[...] = total

    for s in range(NZ):
        at = (z + DZ[s]) % NZ
        share = sh_all[DZ[s], 0, 0:1] + sh_all[DZ[s], 1, 0:1]
        m_line = fm[pl.ds(at, 1), :]
        f_line = share / fs[pl.ds(at, 1), :]
        m_c = jnp.sum(jnp.where(eye(), m_line, 0.0), axis=1, keepdims=True)
        f_c = jnp.sum(jnp.where(eye(), f_line, 0.0), axis=1, keepdims=True)
        cm[s * 128:(s + 1) * 128, :] = jnp.broadcast_to(m_c, (128, 128))
        cf[s * 128:(s + 1) * 128, :] = jnp.broadcast_to(f_c, (128, 128))

    def weigh(t):
        def step(i, carry):
            r0 = pl.multiple_of(i * 64 + t * ROWS_DEV, ROWS_DEV)
            at = pl.ds(r0, ROWS_DEV)
            block = lg[at, :].reshape(ROWS_DEV, VP)
            m = cm[at, 0:1]
            f = cf[at, 0:1]
            pr[t, i // NC, i % NC] = (jnp.exp(block - m) * f).astype(BF16)
            return carry

        lax.fori_loop(0, NZ * NC, step, 0)

    def half(ref, h, q):
        return ref.at[pl.ds(h * 4 + q * 2, 2)]

    ahead, behind, across = (y + 1) % NY, (y + 3) % NY, (y + 2) % NY
    weigh(across)
    for q in range(2):
        send(("far", 1, q), half(pr.at[across], 1, q), far_in.at[0, q], dev(dy=1))
        send(("far", -1, q), half(pr.at[across], 0, q), far_in.at[1, q], dev(dy=-1))
    weigh(ahead)
    for q in range(2):
        send(("near", 1, q), half(pr.at[ahead], 0, q), near_in.at[0, q], dev(dy=1))
    weigh(behind)
    for q in range(2):
        send(("near", -1, q), half(pr.at[behind], 1, q), near_in.at[1, q], dev(dy=-1))
    for q in range(2):
        for sign, t, h, j in ((1, ahead, 1, 0), (-1, behind, 0, 1)):
            arrive(("far", sign, q), far_in.at[j, q])

            def add(i, carry, t=t, h=h, j=j, q=q):
                s = h * 4 + q * 2 + i // NC
                pr[t, s, i % NC] = (pr[t, s, i % NC].astype(F32)
                                    + far_in[j, q, i // NC, i % NC].astype(F32)).astype(BF16)
                return carry

            lax.fori_loop(0, 2 * NC, add, 0)
            send(("sum", sign, q), half(pr.at[t], h, q), sum_in.at[j, q], dev(dy=sign))
    weigh(y)
    for q in range(2):
        for h in range(2):
            near_key, near_j = (("near", 1, q), 0) if h == 0 else (("near", -1, q), 1)
            sum_key, sum_j = (("sum", -1, q), 1) if h == 0 else (("sum", 1, q), 0)
            arrive(near_key, near_in.at[near_j, q])
            arrive(sum_key, sum_in.at[sum_j, q])

            def add(i, carry, h=h, q=q, near_j=near_j, sum_j=sum_j):
                s = h * 4 + q * 2 + i // NC
                mix[s, i % NC] = (pr[y, s, i % NC].astype(F32)
                                  + near_in[near_j, q, i // NC, i % NC].astype(F32)
                                  + sum_in[sum_j, q, i // NC, i % NC].astype(F32)).astype(BF16)
                return carry

            lax.fori_loop(0, 2 * NC, add, 0)
            for i in range(2):
                s = h * 4 + q * 2 + i
                for dc in range(NC):
                    if (s, dc) != (0, 0):
                        dz = DZ[s]
                        send(("rz", (-dz) % NZ, dc), mix.at[s, (c + dc) % NC],
                             out_ref.at[z, c], dev(dz=dz, dc=dc))
    last = pltpu.make_async_copy(mix.at[0, c], out_ref.at[z, c], loc_sem)
    last.start()
    last.wait()
    for dz in range(NZ):
        for dc in range(NC):
            if (dz, dc) != (0, 0):
                arrive(("rz", dz, dc), out_ref.at[(z + dz) % NZ, (c + dc) % NC])
    for copy in sent:
        copy.wait_send()


def spread(mix_ref, out_ref):
    chunks = NZ * NC
    for j in range(chunks):
        start = j * VD
        base, shift = start // 128 * 128, start % 128
        vals = jnp.log(mix_ref[j // NC, j % NC].astype(F32))
        wide = jnp.concatenate([vals, jnp.zeros((ROWS_DEV, 128), F32)], axis=1)
        if shift:
            wide = pltpu.roll(wide, shift, 1)
            lane = lax.broadcasted_iota(jnp.int32, (ROWS_DEV, 128), 1)
            first = jnp.where(lane < shift, out_ref[:, base:base + 128], wide[:, 0:128])
            out_ref[:, base:base + 128] = first
        else:
            out_ref[:, base:base + 128] = wide[:, 0:128]
        end = min(base + wide.shape[1], chunks * VD)
        out_ref[:, base + 128:end] = wide[:, 128:end - base]


def per_device(hidden, norm_gain, head_weight, expert_ids, mix_weight):
    wt_in = jnp.transpose(head_weight.reshape(D, VD))
    vmem = pl.BlockSpec(memory_space=pltpu.VMEM)
    n_sem = len(SEMS)
    returned = pl.pallas_call(
        body,
        out_shape=jax.ShapeDtypeStruct((NZ, NC, ROWS_DEV, VP), BF16),
        in_specs=[vmem, vmem, vmem, vmem, pl.BlockSpec(memory_space=pl.ANY)],
        out_specs=vmem,
        scratch_shapes=[
            pltpu.VMEM((VD, D), BF16),
            pltpu.VMEM((NY, ROWS_DEV, FQ), BF16),
            pltpu.VMEM((NZ, NX, NC, NY, ROWS_DEV, FQ), BF16),
            pltpu.VMEM((NY, 8, 128), F32),
            pltpu.VMEM((NY, 8, 128), F32),
            pltpu.VMEM((NZ, NC, 8, 128), F32),
            pltpu.VMEM((NZ * 128, VP), F32),
            pltpu.VMEM((2, NZ * 128, 128), F32),
            pltpu.VMEM((16, 128), F32),
            pltpu.VMEM((NX, NC, 16, 128), F32),
            pltpu.VMEM((16, 128), F32),
            pltpu.VMEM((NZ, 16, 128), F32),
            pltpu.VMEM((8, 128), F32),
            pltpu.VMEM((8, 128), F32),
            pltpu.VMEM((NZ * 128, 128), F32),
            pltpu.VMEM((NZ * 128, 128), F32),
            pltpu.VMEM((NY, NZ, NC, ROWS_DEV, VP), BF16),
            pltpu.VMEM((2, 2, 2, NC, ROWS_DEV, VP), BF16),
            pltpu.VMEM((2, 2, 2, NC, ROWS_DEV, VP), BF16),
            pltpu.VMEM((2, 2, 2, NC, ROWS_DEV, VP), BF16),
            pltpu.VMEM((NZ, NC, ROWS_DEV, VP), BF16),
            pltpu.SemaphoreType.DMA,
            pltpu.SemaphoreType.DMA,
            pltpu.SemaphoreType.DMA((n_sem,)),
            pltpu.SemaphoreType.DMA((n_sem,)),
        ],
        compiler_params=pltpu.CompilerParams(
            collective_id=0, has_side_effects=True, vmem_limit_bytes=56 * 1024 * 1024),
    )(hidden, norm_gain, expert_ids, mix_weight, wt_in)
    return pl.pallas_call(
        spread,
        out_shape=jax.ShapeDtypeStruct((ROWS_DEV, NZ * NC * VD), F32),
        in_specs=[vmem],
        out_specs=vmem,
    )(returned)


def solution(mesh):
    placed = (
        P("expert", None),
        P(),
        P(None, "tensor", "expert"),
        P("expert", None),
        P("expert", None),
    )
    return jax.shard_map(
        per_device, mesh=mesh, in_specs=placed, out_specs=P("expert", "tensor"), check_vma=False
    )
```

time: 370 us -> 121 us (0.33)
  blocking collectives: 193 us -> 0 us
  Pallas kernels: 0 us -> 118 us
  waiting for transfers between devices: 91.7 us -> 0 us
  local copies, waits for them, and re-layouts: 37.7 us -> 2.7 us
  between operations: 13.6 us -> 0.01 us
  other arithmetic: 13.3 us -> 0 us
  matrix products: 12.2 us -> 0 us
  starting transfers between devices: 8.43 us -> 0 us
    pallas_call x0 -> x2, Pallas kernels: none -> 118 us  [the longest x1 116 us: per_device(): pl.pallas_call(body, out_shape=jax.ShapeDtypeStruct((NZ, NC, ROWS_DEV, VP...]
    pmax x1 -> x0, blocking collectives: 75.2 us -> none  [per_device(): lax.pmax(jnp.where(owned, row_top[None, :], FAR), ('expert', 'tensor'))]
    psum x1 -> x0, blocking collectives: 73.4 us -> none  [per_device(): lax.psum(jnp.where(owned, jnp.sum(raised, axis=1)[None, :], 0.0), ('exper...]
    all_to_all x1 -> x0, waiting for transfers between devices: 50.9 us -> none  [per_device(): lax.all_to_all(probs, 'expert', split_axis=0, concat_axis=1, tiled=True)]
    all_gather x1 -> x0, blocking collectives: 44.2 us -> none  [per_device(): lax.all_gather(expert_ids.astype(jnp.bfloat16), 'expert', axis=0, tiled=T...]
    all_gather x1 -> x0, waiting for transfers between devices: 40.1 us -> none  [per_device(): lax.all_gather(hidden, 'expert', axis=0, tiled=True)]
    gather x3 -> x0, local copies, waits for them, and re-layouts: 23.5 us -> none  [the longest x1 19.4 us: per_device(): slot_rows = all_rows[source_row[:capacity]]]
    dot_general x1 -> x0, matrix products: 12.2 us -> none  [per_device(): logits = jnp.dot(normed, local_head, preferred_element_type=jnp.float32)]
  transfers between devices with their start and end apart: 2 -> 0, of which waited for: 2 -> 0; matrix products, arithmetic and copies ran while one was open for 2% -> 0% of each run, Pallas kernels for 0% -> 0%
where the time goes in v1:
time: 121 us
  Pallas kernels  118 us (98%)
  local copies, waits for them, and re-layouts  2.7 us (2%)
    pallas_call x1, Pallas kernels, per_device(): pl.pallas_call(body, out_shape=jax.ShapeDtypeStruct((NZ, NC, ROWS_DEV, VP...  116 us
    unnamed x2, local copies, waits for them, and re-layouts  2.7 us

profile of v1, /device:TPU:1, one launch (start us, length us, event | category | flops | bytes accessed | tf_op | source)
XLA Modules:
  0.0 120.7 jit_solution(1141275672547478996)
XLA Ops:
  0.0 1.4 %copy.6.ids_ref = s32[16,2]{1,0:T(8,128)} copy(s32[16,2]{0,1:T(2,128)} %param.8) | data formatting | bytes 256 | tf_op args[3]
  1.4 1.3 %copy.7.mw_ref = s32[16,2]{1,0:T(8,128)} copy(s32[16,2]{0,1:T(2,128)} %param.9) | data formatting | bytes 256 | tf_op args[4]
  2.7 115.7 %shard_map.55.mix_ref = bf16[8,2,16,1024]{3,2,1,0:T(8,128)(2,1)} custom-call(bf16[16,4096]{1,0:T(8,128)(2,1)} %h_ref.1, f32[4,4096]{1,0:T(4,128)} %g_ref.1, s32[16,2]{1,0:T(8,128)} %copy.6.ids_ref, s32[16,2]{1,0:T(8,128)} %copy.7.mw_ref, bf16[1002,4096]{1,0:T(8,128)(2,1)} %bitcast.3), custom_call_target="tpu_custom_call" | custom-call | tf_op jit(solution)/shard_map/pallas_call | solution.py:421
  118.4 2.3 %shard_map.56 = f32[16,16032]{1,0:T(8,128)} custom-call(bf16[8,2,16,1024]{3,2,1,0:T(8,128)(2,1)} %shard_map.55.mix_ref), custom_call_target="tpu_custom_call" | custom-call | tf_op jit(solution)/shard_map/pallas_call | solution.py:456

commit v2 on v1

v2 whole, which is shorter than its diff:
```python
import jax
import jax.numpy as jnp
from jax import lax
from jax.experimental import pallas as pl
from jax.experimental.pallas import tpu as pltpu
from jax.sharding import PartitionSpec as P

EPS = 1e-05
FAR = -1e30
LOG2E = 1.4426950408889634
NX, NY, NZ, NC = 4, 4, 8, 2
ROWS_DEV = 16
D = 4096
FQ = D // NX
VD = 1002
VP = 1024
FA = 640
FB = FQ - FA
MESH = pl.DeviceIdType.MESH
F32 = jnp.float32
BF16 = jnp.bfloat16

SLOT = {0: 0, 7: 1, 1: 2, 6: 3, 2: 4, 5: 5, 3: 6, 4: 7}
DZ = {s: d for d, s in SLOT.items()}


def sem_table():
    names = []
    names += [("y", k) for k in range(1, NY)]
    names += [("sy", k) for k in range(1, NY)]
    names += [("sz", dz, dc) for dz in range(NZ) for dc in range(NC) if (dz, dc) != (0, 0)]
    names += [("az", dz) for dz in range(1, NZ)]
    names += [("ax", dz, dx) for dz in range(NZ) for dx in range(1, NX)]
    names += [("bx", dx) for dx in range(1, NX)]
    names += [("bz", dz, dx) for dz in range(1, NZ) for dx in range(NX)]
    names += [("cc", dz, dx) for dz in range(NZ) for dx in range(NX)]
    names += [("tx", dx, dc) for dx in range(NX) for dc in range(NC) if (dx, dc) != (0, 0)]
    names += [("tz", dz) for dz in range(1, NZ)]
    names += [(kind, sign, q) for kind in ("far", "near", "sum") for sign in (1, -1) for q in range(4)]
    names += [("rz", dz, dc) for dz in range(NZ) for dc in range(NC) if (dz, dc) != (0, 0)]
    return {name: i for i, name in enumerate(names)}


SEMS = sem_table()


def body(h_ref, g_ref, ids_ref, mw_ref, w_ref, out_ref,
         wt, n4, gat, line, sh_src, sh_y, sh_all, lg, st_own, st_x, st_zsrc, st_z,
         fm, fs, pr, far_in, near_in, sum_in, mix, w_sem, loc_sem, ss, rs):
    me = lax.axis_index("expert")
    x = lax.axis_index("tensor")
    y = me // (NZ * NC)
    z = (me // NC) % NZ
    c = me % NC

    def dev(dx=0, dy=0, dz=0, dc=0):
        yy = (y + dy) % NY
        zz = (z + dz) % NZ
        cc = (c + dc) % NC
        return ((yy * NZ + zz) * NC + cc, (x + dx) % NX)

    sent = []

    def send(key, src, dst, to):
        k = SEMS[key]
        copy = pltpu.make_async_remote_copy(
            src_ref=src, dst_ref=dst, send_sem=ss.at[k], recv_sem=rs.at[k],
            device_id=to, device_id_type=MESH)
        copy.start()
        sent.append(copy)

    def arrive(key, dst):
        k = SEMS[key]
        pltpu.make_async_remote_copy(
            src_ref=dst, dst_ref=dst, send_sem=ss.at[k], recv_sem=rs.at[k],
            device_id=dev(dc=1), device_id_type=MESH).wait_recv()

    w_copy = pltpu.make_async_copy(w_ref, wt, w_sem)
    w_copy.start()

    peers = [dev(dy=k) for k in range(1, NY)]
    peers += [dev(dz=1), dev(dz=-1), dev(dx=1), dev(dx=-1), dev(dc=1)]
    barrier = pltpu.get_barrier_semaphore()
    for peer in peers:
        pl.semaphore_signal(barrier, inc=1, device_id=peer, device_id_type=MESH)

    h_all = h_ref[...].astype(F32)
    rms = jnp.sqrt(jnp.mean(h_all * h_all, axis=1, keepdims=True) + EPS)
    cols = pl.ds(pl.multiple_of(x * FQ, FQ), FQ)
    h_q = h_ref[:, cols].astype(F32) / rms
    for e in range(NY):
        n4[e] = (h_q * g_ref[pl.ds(e, 1), cols]).astype(BF16)
    counts = mw_ref[...].astype(F32)
    shares = counts / (counts[0:1] + counts[1:2])
    ids = ids_ref[...]
    line[...] = jnp.zeros_like(line)
    for e in range(NY):
        line[e:e + 1, 0:ROWS_DEV] = jnp.sum(jnp.where(ids == e, shares, 0.0), axis=0, keepdims=True)
    lines = pltpu.roll(line[...], c * 64 + y * ROWS_DEV, 1)
    for e in range(NY):
        sh_src[e] = jnp.broadcast_to(lines[e:e + 1], (8, 128))

    pl.semaphore_wait(barrier, len(peers))

    for k in (2, 1, 3):
        send(("y", k), n4.at[(y + k) % NY], gat.at[0, x, c, y], dev(dy=k))
    for k in (2, 1, 3):
        send(("sy", k), sh_src.at[(y + k) % NY], sh_y.at[k], dev(dy=k))
    own = pltpu.make_async_copy(n4.at[y], gat.at[0, x, c, y], loc_sem)
    own.start()
    own.wait()
    for k in (1, 3, 2):
        arrive(("y", k), gat.at[0, x, c, (y - k) % NY])

    def unit(dz, dx):
        return gat.at[SLOT[dz], (x + dx) % NX, c]

    def part_a(dz, dx):
        return gat.at[SLOT[dz], (x + dx) % NX, c, :, :, pl.ds(0, FA)]

    def part_b(dz, dx):
        return gat.at[SLOT[dz], (x + dx) % NX, c, :, :, pl.ds(FA, FB)]

    def a_along_z(dz, step):
        to = (dz - step) % NZ
        send(("az", to), part_a(dz, 0), part_a(to, 0), dev(dz=step))

    def a_along_x(dz):
        send(("ax", dz, 3), part_a(dz, 0), part_a(dz, 0), dev(dx=1))
        send(("ax", dz, 1), part_a(dz, 0), part_a(dz, 0), dev(dx=-1))

    def a_opposite(dz):
        for dx in (3, 1):
            arrive(("ax", dz, dx), part_a(dz, dx))
            if dx == (3 if dz % 2 == 0 else 1):
                step = 1 if dx == 3 else -1
                send(("ax", dz, 2), part_a(dz, dx), part_a(dz, dx), dev(dx=step))

    def b_along_z(dz, dx, step):
        to = (dz - step) % NZ
        send(("bz", to, dx), part_b(dz, dx), part_b(to, dx), dev(dz=step))

    def to_sibling(dz, dx):
        send(("cc", dz, dx), unit(dz, dx), unit(dz, dx), dev(dc=1))

    def right_hops(dx):
        return 4 if dx in (0, 1) else 3

    def b_round(k, dx):
        if k <= right_hops(dx):
            arrive(("bz", NZ - k, dx), part_b(NZ - k, dx))
            if k < right_hops(dx):
                b_along_z(NZ - k, dx, 1)
        if k <= 7 - right_hops(dx):
            arrive(("bz", k, dx), part_b(k, dx))
            if k < 7 - right_hops(dx):
                b_along_z(k, dx, -1)

    def eye():
        return (lax.broadcasted_iota(jnp.int32, (128, 128), 0)
                == lax.broadcasted_iota(jnp.int32, (128, 128), 1))

    def logits(g, n):
        rows = 2 * 128
        lo, hi = ((0, 512), (512, VD))[n]
        acc = jnp.zeros((rows, hi - lo), F32)
        for xi in range(NX):
            lhs = gat[2 * g:2 * g + 2, xi].reshape(rows, FQ)
            acc += lax.dot_general(
                lhs, wt[lo:hi, xi * FQ:(xi + 1) * FQ],
                (((1,), (1,)), ((), ())), preferred_element_type=F32)
        acc = acc * LOG2E
        if n == 1:
            acc = jnp.concatenate([acc, jnp.full((rows, VP - VD), FAR, F32)], axis=1)
        lg[g * rows:(g + 1) * rows, lo:lo + 512] = acc

    def stats(g):
        rows = 2 * 128
        at = slice(g * rows, (g + 1) * rows)
        lanes = [slice(j * 128, (j + 1) * 128) for j in range(VP // 128)]
        top = lg[at, lanes[0]]
        for ln in lanes[1:]:
            top = jnp.maximum(top, lg[at, ln])
        top = jnp.broadcast_to(jnp.max(top, axis=1, keepdims=True), (rows, 128))
        total = jnp.exp2(lg[at, lanes[0]] - top)
        for ln in lanes[1:]:
            total += jnp.exp2(lg[at, ln] - top)
        total = jnp.broadcast_to(jnp.sum(total, axis=1, keepdims=True), (rows, 128))
        for i in range(2):
            where = (z + DZ[2 * g + i]) % NZ
            for j, col in enumerate((top, total)):
                st_own[pl.ds(j * 8 + where, 1), :] = jnp.sum(
                    jnp.where(eye(), col[i * 128:(i + 1) * 128], 0.0), axis=0, keepdims=True)

    a_along_z(0, 1)
    a_along_z(0, -1)
    send(("bx", 3), part_b(0, 0), part_b(0, 0), dev(dx=1))
    send(("bx", 1), part_b(0, 0), part_b(0, 0), dev(dx=-1))
    a_along_x(0)
    b_along_z(0, 0, 1)
    b_along_z(0, 0, -1)
    to_sibling(0, 0)

    for dx in (3, 1, 2):
        arrive(("bx", dx), part_b(0, dx))
        if dx == 3:
            send(("bx", 2), part_b(0, 3), part_b(0, 3), dev(dx=1))
        b_along_z(0, dx, 1)
        b_along_z(0, dx, -1)

    for k in (1, 3, 2):
        arrive(("sy", k), sh_y.at[k])
    sh_all[0, c] = sh_src[y] + sh_y[1] + sh_y[2] + sh_y[3]

    def finish_x(dz):
        for dx in range(1, NX):
            if dx == 2:
                arrive(("ax", dz, 2), part_a(dz, 2))
            to_sibling(dz, dx)

    def from_sibling(dz):
        for dx in range(NX):
            arrive(("cc", dz, dx), gat.at[SLOT[dz], (x + dx) % NX, 1 - c])

    def a_round(k):
        arrive(("az", NZ - k), part_a(NZ - k, 0))
        if k < 4:
            a_along_z(NZ - k, 1)
        a_along_x(NZ - k)
        if k < 4:
            arrive(("az", k), part_a(k, 0))
            if k < 3:
                a_along_z(k, -1)
            a_along_x(k)

    def b_all(k):
        for dx in range(NX):
            b_round(k, dx)

    def places(k):
        return {0: (0,), 4: (4,)}.get(k, (NZ - k, k))

    def opposite(k):
        for dz in places(k):
            a_opposite(dz)

    def finish(k):
        for dz in places(k):
            if dz:
                to_sibling(dz, 0)
            finish_x(dz)

    a_round(1)
    opposite(0)
    a_round(2)
    b_all(1)
    opposite(1)
    finish(0)
    a_round(3)
    opposite(2)
    b_all(2)
    finish(1)
    a_round(4)
    w_copy.wait()
    from_sibling(0)
    from_sibling(7)
    logits(0, 0)
    opposite(3)
    b_all(3)
    logits(0, 1)
    finish(2)
    opposite(4)
    b_all(4)
    stats(0)
    from_sibling(1)
    from_sibling(6)
    logits(1, 0)
    finish(3)
    finish(4)
    logits(1, 1)
    stats(1)
    from_sibling(2)
    from_sibling(5)
    logits(2, 0)
    logits(2, 1)
    stats(2)
    from_sibling(3)
    from_sibling(4)
    logits(3, 0)
    logits(3, 1)
    stats(3)

    def merge(parts):
        top = parts[0][0]
        for m, _ in parts[1:]:
            top = jnp.maximum(top, m)
        total = jnp.zeros_like(top)
        for m, s in parts:
            total += s * jnp.exp2(m - top)
        return top, total

    near_peers = [(a, b) for a in range(NX) for b in range(NC) if (a, b) != (0, 0)]
    for a, b in near_peers:
        send(("tx", (-a) % NX, b), st_own, st_x.at[(-a) % NX, b], dev(dx=a, dc=b))
    for dz in range(NZ):
        for dc in range(NC):
            if (dz, dc) != (0, 0):
                send(("sz", (-dz) % NZ, dc), sh_all.at[0, c], sh_all.at[(-dz) % NZ, c],
                     dev(dz=dz, dc=dc))
    parts = [(st_own[0:8], st_own[8:16])]
    for a, b in near_peers:
        arrive(("tx", a, b), st_x.at[a, b])
        parts.append((st_x[a, b, 0:8], st_x[a, b, 8:16]))
    top, total = merge(parts)
    st_zsrc[0:8] = top
    st_zsrc[8:16] = total
    for k in range(1, NZ):
        send(("tz", (-k) % NZ), st_zsrc, st_z.at[(-k) % NZ], dev(dz=k))
    parts = [(top, total)]
    for k in range(1, NZ):
        arrive(("tz", k), st_z.at[k])
        parts.append((st_z[k, 0:8], st_z[k, 8:16]))
    top, total = merge(parts)
    fm[...] = top
    fs[...] = total
    for dz in range(NZ):
        for dc in range(NC):
            if (dz, dc) != (0, 0):
                arrive(("sz", dz, dc), sh_all.at[dz, (c + dc) % NC])
    def weigh(s):
        at = (z + DZ[s]) % NZ
        share = sh_all[DZ[s], 0, 0:1] + sh_all[DZ[s], 1, 0:1]
        m_line = fm[pl.ds(at, 1), :]
        f_line = share / fs[pl.ds(at, 1), :]
        m_c = jnp.sum(jnp.where(eye(), m_line, 0.0), axis=1, keepdims=True)
        f_c = jnp.sum(jnp.where(eye(), f_line, 0.0), axis=1, keepdims=True)
        m_c = jnp.broadcast_to(m_c, (128, 128))
        f_c = jnp.broadcast_to(f_c, (128, 128))
        for j in range(VP // 128):
            ln = slice(j * 128, (j + 1) * 128)
            p = (jnp.exp2(lg[s * 128:(s + 1) * 128, ln] - m_c) * f_c).astype(BF16)
            for b in range(NC * NY):
                pr[b % NY, s, b // NY, :, ln] = p[b * ROWS_DEV:(b + 1) * ROWS_DEV]

    ahead, behind, across = (y + 1) % NY, (y + 3) % NY, (y + 2) % NY

    def first_sends(q):
        for s in (q, 4 + q):
            weigh(s)
        send(("far", 1, q), pr.at[across, 4 + q], far_in.at[0, q], dev(dy=1))
        send(("far", -1, q), pr.at[across, q], far_in.at[1, q], dev(dy=-1))
        send(("near", 1, q), pr.at[ahead, q], near_in.at[0, q], dev(dy=1))
        send(("near", -1, q), pr.at[behind, 4 + q], near_in.at[1, q], dev(dy=-1))

    def relay(q):
        for sign, t, s, j in ((1, ahead, 4 + q, 0), (-1, behind, q, 1)):
            arrive(("far", sign, q), far_in.at[j, q])
            pr[t, s] = (pr[t, s].astype(F32) + far_in[j, q].astype(F32)).astype(BF16)
            send(("sum", sign, q), pr.at[t, s], sum_in.at[j, q], dev(dy=sign))

    def combine(q):
        for s, near_j, sum_j in ((q, 0, 1), (4 + q, 1, 0)):
            arrive(("near", 1 - 2 * near_j, q), near_in.at[near_j, q])
            arrive(("sum", 1 - 2 * sum_j, q), sum_in.at[sum_j, q])
            mix[s] = (pr[y, s].astype(F32) + near_in[near_j, q].astype(F32)
                      + sum_in[sum_j, q].astype(F32)).astype(BF16)
            dz = DZ[s]
            for dc in range(NC):
                if (dz, dc) != (0, 0):
                    send(("rz", (-dz) % NZ, dc), mix.at[s, (c + dc) % NC],
                         out_ref.at[z, c], dev(dz=dz, dc=dc))

    first_sends(0)
    first_sends(1)
    for q in range(4):
        relay(q)
        if q < 2:
            first_sends(q + 2)
        if q:
            combine(q - 1)
    combine(3)
    last = pltpu.make_async_copy(mix.at[0, c], out_ref.at[z, c], loc_sem)
    last.start()
    last.wait()
    for dz in range(NZ):
        for dc in range(NC):
            if (dz, dc) != (0, 0):
                arrive(("rz", dz, dc), out_ref.at[(z + dz) % NZ, (c + dc) % NC])
    for copy in sent:
        copy.wait_send()


def spread(mix_ref, out_ref):
    chunks = NZ * NC
    for j in range(chunks):
        start = j * VD
        base, shift = start // 128 * 128, start % 128
        vals = jnp.log(mix_ref[j // NC, j % NC].astype(F32))
        wide = jnp.concatenate([vals, jnp.zeros((ROWS_DEV, 128), F32)], axis=1)
        if shift:
            wide = pltpu.roll(wide, shift, 1)
            lane = lax.broadcasted_iota(jnp.int32, (ROWS_DEV, 128), 1)
            first = jnp.where(lane < shift, out_ref[:, base:base + 128], wide[:, 0:128])
            out_ref[:, base:base + 128] = first
        else:
            out_ref[:, base:base + 128] = wide[:, 0:128]
        end = min(base + wide.shape[1], chunks * VD)
        out_ref[:, base + 128:end] = wide[:, 128:end - base]


def per_device(hidden, norm_gain, head_weight, expert_ids, mix_weight):
    wt_in = jnp.transpose(head_weight.reshape(D, VD))
    vmem = pl.BlockSpec(memory_space=pltpu.VMEM)
    n_sem = len(SEMS)
    returned = pl.pallas_call(
        body,
        out_shape=jax.ShapeDtypeStruct((NZ, NC, ROWS_DEV, VP), BF16),
        in_specs=[vmem, vmem, vmem, vmem, pl.BlockSpec(memory_space=pl.ANY)],
        out_specs=vmem,
        scratch_shapes=[
            pltpu.VMEM((VD, D), BF16),
            pltpu.VMEM((NY, ROWS_DEV, FQ), BF16),
            pltpu.VMEM((NZ, NX, NC, NY, ROWS_DEV, FQ), BF16),
            pltpu.VMEM((8, 128), F32),
            pltpu.VMEM((NY, 8, 128), F32),
            pltpu.VMEM((NY, 8, 128), F32),
            pltpu.VMEM((NZ, NC, 8, 128), F32),
            pltpu.VMEM((NZ * 128, VP), F32),
            pltpu.VMEM((16, 128), F32),
            pltpu.VMEM((NX, NC, 16, 128), F32),
            pltpu.VMEM((16, 128), F32),
            pltpu.VMEM((NZ, 16, 128), F32),
            pltpu.VMEM((8, 128), F32),
            pltpu.VMEM((8, 128), F32),
            pltpu.VMEM((NY, NZ, NC, ROWS_DEV, VP), BF16),
            pltpu.VMEM((2, 4, NC, ROWS_DEV, VP), BF16),
            pltpu.VMEM((2, 4, NC, ROWS_DEV, VP), BF16),
            pltpu.VMEM((2, 4, NC, ROWS_DEV, VP), BF16),
            pltpu.VMEM((NZ, NC, ROWS_DEV, VP), BF16),
            pltpu.SemaphoreType.DMA,
            pltpu.SemaphoreType.DMA,
            pltpu.SemaphoreType.DMA((n_sem,)),
            pltpu.SemaphoreType.DMA((n_sem,)),
        ],
        compiler_params=pltpu.CompilerParams(
            collective_id=0, has_side_effects=True, vmem_limit_bytes=56 * 1024 * 1024),
    )(hidden, norm_gain, expert_ids.T, mix_weight.T, wt_in)
    return pl.pallas_call(
        spread,
        out_shape=jax.ShapeDtypeStruct((ROWS_DEV, NZ * NC * VD), F32),
        in_specs=[vmem],
        out_specs=vmem,
    )(returned)


def solution(mesh):
    placed = (
        P("expert", None),
        P(),
        P(None, "tensor", "expert"),
        P("expert", None),
        P("expert", None),
    )
    return jax.shard_map(
        per_device, mesh=mesh, in_specs=placed, out_specs=P("expert", "tensor"), check_vma=False
    )
```

time: 121 us -> 91.9 us (0.76)
  Pallas kernels: 118 us -> 91.7 us
  local copies, waits for them, and re-layouts: 2.7 us -> 0 us
    pallas_call x1, Pallas kernels: 116 us -> 89.4 us  [per_device(): pl.pallas_call(body, out_shape=jax.ShapeDtypeStruct((NZ, NC, ROWS_DEV, VP...]
    unnamed x2 -> x0, local copies, waits for them, and re-layouts: 2.7 us -> none
where the time goes in v2:
time: 91.9 us; the launch traced here: 91.7 us
  Pallas kernels  91.7 us (100%)
    pallas_call x1, Pallas kernels, per_device(): pl.pallas_call(body, out_shape=jax.ShapeDtypeStruct((NZ, NC, ROWS_DEV, VP...  89.4 us
    pallas_call x1, Pallas kernels, per_device(): pl.pallas_call(spread, out_shape=jax.ShapeDtypeStruct((ROWS_DEV, NZ * NC...  2.35 us

profile of v2, /device:TPU:1, one launch (start us, length us, event | category | flops | bytes accessed | tf_op | source)
XLA Modules:
  0.0 91.7 jit_solution(6019178402347545519)
XLA Ops:
  0.0 89.4 %shard_map.55.mix_ref = bf16[8,2,16,1024]{3,2,1,0:T(8,128)(2,1)} custom-call(bf16[16,4096]{1,0:T(8,128)(2,1)} %h_ref.1, f32[4,4096]{1,0:T(4,128)} %g_ref.1, s32[2,16]{1,0:T(2,128)} %bitcast.6, s32[2,16]{1,0:T(2,128)} %bitcast.7, bf16[1002,4096]{1,0:T(8,128)(2,1)} %bitcast.5), custom_call_target="tpu_custom_call" | custom-call | tf_op jit(solution)/shard_map/pallas_call | solution.py:415
  89.4 2.3 %shard_map.56 = f32[16,16032]{1,0:T(8,128)} custom-call(bf16[8,2,16,1024]{3,2,1,0:T(8,128)(2,1)} %shard_map.55.mix_ref), custom_call_target="tpu_custom_call" | custom-call | tf_op jit(solution)/shard_map/pallas_call | solution.py:448

commit v3 on v2

--- a/solution.py
+++ b/solution.py
@@ -29,14 +29,15 @@
     names += [("y", k) for k in range(1, NY)]
     names += [("sy", k) for k in range(1, NY)]
     names += [("sz", dz, dc) for dz in range(NZ) for dc in range(NC) if (dz, dc) != (0, 0)]
-    names += [("az", dz) for dz in range(1, NZ)]
+    names += [("az", dz, k) for dz in range(1, NZ) for k in range(NY)]
     names += [("ax", dz, dx) for dz in range(NZ) for dx in range(1, NX)]
     names += [("bx", dx) for dx in range(1, NX)]
     names += [("bz", dz, dx) for dz in range(1, NZ) for dx in range(NX)]
     names += [("cc", dz, dx) for dz in range(NZ) for dx in range(NX)]
     names += [("tx", dx, dc) for dx in range(NX) for dc in range(NC) if (dx, dc) != (0, 0)]
     names += [("tz", dz) for dz in range(1, NZ)]
-    names += [(kind, sign, q) for kind in ("far", "near", "sum") for sign in (1, -1) for q in range(4)]
+    names += [("ye", k, s) for k in range(1, NY) for s in range(NZ)]
+    names += [("yf", k) for k in range(1, NY)]
     names += [("rz", dz, dc) for dz in range(NZ) for dc in range(NC) if (dz, dc) != (0, 0)]
     return {name: i for i, name in enumerate(names)}
 
@@ -46,7 +47,7 @@
 
 def body(h_ref, g_ref, ids_ref, mw_ref, w_ref, out_ref,
          wt, n4, gat, line, sh_src, sh_y, sh_all, lg, st_own, st_x, st_zsrc, st_z,
-         fm, fs, pr, far_in, near_in, sum_in, mix, w_sem, loc_sem, ss, rs):
+         sh_abs, f_own, f_in, pr, y_in, mix, w_sem, loc_sem, ss, rs):
     me = lax.axis_index("expert")
     x = lax.axis_index("tensor")
     y = me // (NZ * NC)
@@ -106,12 +107,6 @@
         send(("y", k), n4.at[(y + k) % NY], gat.at[0, x, c, y], dev(dy=k))
     for k in (2, 1, 3):
         send(("sy", k), sh_src.at[(y + k) % NY], sh_y.at[k], dev(dy=k))
-    own = pltpu.make_async_copy(n4.at[y], gat.at[0, x, c, y], loc_sem)
-    own.start()
-    own.wait()
-    for k in (1, 3, 2):
-        arrive(("y", k), gat.at[0, x, c, (y - k) % NY])
-
     def unit(dz, dx):
         return gat.at[SLOT[dz], (x + dx) % NX, c]
 
@@ -121,9 +116,12 @@
     def part_b(dz, dx):
         return gat.at[SLOT[dz], (x + dx) % NX, c, :, :, pl.ds(FA, FB)]
 
-    def a_along_z(dz, step):
+    def piece(dz, k):
+        return gat.at[SLOT[dz], x, c, (y - k) % NY, :, pl.ds(0, FA)]
+
+    def a_along_z(dz, k, step):
         to = (dz - step) % NZ
-        send(("az", to), part_a(dz, 0), part_a(to, 0), dev(dz=step))
+        send(("az", to, k), piece(dz, k), piece(to, k), dev(dz=step))
 
     def a_along_x(dz):
         send(("ax", dz, 3), part_a(dz, 0), part_a(dz, 0), dev(dx=1))
@@ -182,9 +180,18 @@
         for ln in lanes[1:]:
             top = jnp.maximum(top, lg[at, ln])
         top = jnp.broadcast_to(jnp.max(top, axis=1, keepdims=True), (rows, 128))
-        total = jnp.exp2(lg[at, lanes[0]] - top)
-        for ln in lanes[1:]:
-            total += jnp.exp2(lg[at, ln] - top)
+        total = jnp.zeros((rows, 128), F32)
+        for ln in lanes:
+            e = jnp.exp2(lg[at, ln] - top)
+            total += e
+            low = e.astype(BF16)
+            for b in range(2 * NC * NY):
+                i, cc, yy = b // (NC * NY), b // NY % NC, b % NY
+                pr[yy, 2 * g + i, cc, :, ln] = low[b * ROWS_DEV:(b + 1) * ROWS_DEV]
+        for i in range(2):
+            for k in (2, 1, 3):
+                s = 2 * g + i
+                send(("ye", (-k) % NY, s), pr.at[(y + k) % NY, s], y_in.at[(-k) % NY, s], dev(dy=k))
         total = jnp.broadcast_to(jnp.sum(total, axis=1, keepdims=True), (rows, 128))
         for i in range(2):
             where = (z + DZ[2 * g + i]) % NZ
@@ -192,8 +199,12 @@
                 st_own[pl.ds(j * 8 + where, 1), :] = jnp.sum(
                     jnp.where(eye(), col[i * 128:(i + 1) * 128], 0.0), axis=0, keepdims=True)
 
-    a_along_z(0, 1)
-    a_along_z(0, -1)
+    gat[0, x, c, y] = n4[y]
+    for k in (0, 1, 3, 2):
+        if k:
+            arrive(("y", k), gat.at[0, x, c, (y - k) % NY])
+        a_along_z(0, k, 1)
+        a_along_z(0, k, -1)
     send(("bx", 3), part_b(0, 0), part_b(0, 0), dev(dx=1))
     send(("bx", 1), part_b(0, 0), part_b(0, 0), dev(dx=-1))
     a_along_x(0)
@@ -223,14 +234,15 @@
             arrive(("cc", dz, dx), gat.at[SLOT[dz], (x + dx) % NX, 1 - c])
 
     def a_round(k):
-        arrive(("az", NZ - k), part_a(NZ - k, 0))
-        if k < 4:
-            a_along_z(NZ - k, 1)
+        for p in (0, 1, 3, 2):
+            arrive(("az", NZ - k, p), piece(NZ - k, p))
+            if k < 4:
+                a_along_z(NZ - k, p, 1)
+                arrive(("az", k, p), piece(k, p))
+                if k < 3:
+                    a_along_z(k, p, -1)
         a_along_x(NZ - k)
         if k < 4:
-            arrive(("az", k), part_a(k, 0))
-            if k < 3:
-                a_along_z(k, -1)
             a_along_x(k)
 
     def b_all(k):
@@ -286,6 +298,11 @@
     stats(2)
     from_sibling(3)
     from_sibling(4)
+    for dz in range(NZ):
+        for dc in range(NC):
+            if (dz, dc) != (0, 0):
+                send(("sz", (-dz) % NZ, dc), sh_all.at[0, c], sh_all.at[(-dz) % NZ, c],
+                     dev(dz=dz, dc=dc))
     logits(3, 0)
     logits(3, 1)
     stats(3)
@@ -302,11 +319,6 @@
     near_peers = [(a, b) for a in range(NX) for b in range(NC) if (a, b) != (0, 0)]
     for a, b in near_peers:
         send(("tx", (-a) % NX, b), st_own, st_x.at[(-a) % NX, b], dev(dx=a, dc=b))
-    for dz in range(NZ):
-        for dc in range(NC):
-            if (dz, dc) != (0, 0):
-                send(("sz", (-dz) % NZ, dc), sh_all.at[0, c], sh_all.at[(-dz) % NZ, c],
-                     dev(dz=dz, dc=dc))
     parts = [(st_own[0:8], st_own[8:16])]
     for a, b in near_peers:
         arrive(("tx", a, b), st_x.at[a, b])
@@ -321,64 +333,44 @@
         arrive(("tz", k), st_z.at[k])
         parts.append((st_z[k, 0:8], st_z[k, 8:16]))
     top, total = merge(parts)
-    fm[...] = top
-    fs[...] = total
     for dz in range(NZ):
         for dc in range(NC):
             if (dz, dc) != (0, 0):
                 arrive(("sz", dz, dc), sh_all.at[dz, (c + dc) % NC])
-    def weigh(s):
-        at = (z + DZ[s]) % NZ
-        share = sh_all[DZ[s], 0, 0:1] + sh_all[DZ[s], 1, 0:1]
-        m_line = fm[pl.ds(at, 1), :]
-        f_line = share / fs[pl.ds(at, 1), :]
-        m_c = jnp.sum(jnp.where(eye(), m_line, 0.0), axis=1, keepdims=True)
-        f_c = jnp.sum(jnp.where(eye(), f_line, 0.0), axis=1, keepdims=True)
-        m_c = jnp.broadcast_to(m_c, (128, 128))
-        f_c = jnp.broadcast_to(f_c, (128, 128))
+        sh_abs[pl.ds((z + dz) % NZ, 1), :] = sh_all[dz, 0, 0:1] + sh_all[dz, 1, 0:1]
+    f_own[...] = sh_abs[...] * jnp.exp2(st_own[0:8] - top) / total
+    for k in (2, 1, 3):
+        send(("yf", (-k) % NY), f_own, f_in.at[(-k) % NY], dev(dy=k))
+    for k in range(1, NY):
+        arrive(("yf", k), f_in.at[k])
+
+    lane = lax.broadcasted_iota(jnp.int32, (NC * ROWS_DEV, 128), 1)
+    row = lax.broadcasted_iota(jnp.int32, (NC * ROWS_DEV, 128), 0)
+    take = lane == row // ROWS_DEV * 64 + y * ROWS_DEV + row % ROWS_DEV
+
+    def mixing(s):
+        dz = DZ[s]
+        at = pl.ds((z + dz) % NZ, 1)
+        for k in range(1, NY):
+            arrive(("ye", k, s), y_in.at[k, s])
+        cols = []
+        for k in range(NY):
+            factors = f_in[k, at, :] if k else f_own[at, :]
+            col = jnp.sum(jnp.where(take, factors, 0.0), axis=1, keepdims=True)
+            cols.append(jnp.broadcast_to(col, (NC * ROWS_DEV, 128)))
         for j in range(VP // 128):
             ln = slice(j * 128, (j + 1) * 128)
-            p = (jnp.exp2(lg[s * 128:(s + 1) * 128, ln] - m_c) * f_c).astype(BF16)
-            for b in range(NC * NY):
-                pr[b % NY, s, b // NY, :, ln] = p[b * ROWS_DEV:(b + 1) * ROWS_DEV]
-
-    ahead, behind, across = (y + 1) % NY, (y + 3) % NY, (y + 2) % NY
-
-    def first_sends(q):
-        for s in (q, 4 + q):
-            weigh(s)
-        send(("far", 1, q), pr.at[across, 4 + q], far_in.at[0, q], dev(dy=1))
-        send(("far", -1, q), pr.at[across, q], far_in.at[1, q], dev(dy=-1))
-        send(("near", 1, q), pr.at[ahead, q], near_in.at[0, q], dev(dy=1))
-        send(("near", -1, q), pr.at[behind, 4 + q], near_in.at[1, q], dev(dy=-1))
-
-    def relay(q):
-        for sign, t, s, j in ((1, ahead, 4 + q, 0), (-1, behind, q, 1)):
-            arrive(("far", sign, q), far_in.at[j, q])
-            pr[t, s] = (pr[t, s].astype(F32) + far_in[j, q].astype(F32)).astype(BF16)
-            send(("sum", sign, q), pr.at[t, s], sum_in.at[j, q], dev(dy=sign))
-
-    def combine(q):
-        for s, near_j, sum_j in ((q, 0, 1), (4 + q, 1, 0)):
-            arrive(("near", 1 - 2 * near_j, q), near_in.at[near_j, q])
-            arrive(("sum", 1 - 2 * sum_j, q), sum_in.at[sum_j, q])
-            mix[s] = (pr[y, s].astype(F32) + near_in[near_j, q].astype(F32)
-                      + sum_in[sum_j, q].astype(F32)).astype(BF16)
-            dz = DZ[s]
-            for dc in range(NC):
-                if (dz, dc) != (0, 0):
-                    send(("rz", (-dz) % NZ, dc), mix.at[s, (c + dc) % NC],
-                         out_ref.at[z, c], dev(dz=dz, dc=dc))
-
-    first_sends(0)
-    first_sends(1)
-    for q in range(4):
-        relay(q)
-        if q < 2:
-            first_sends(q + 2)
-        if q:
-            combine(q - 1)
-    combine(3)
+            mixed = pr[y, s, :, :, ln].reshape(NC * ROWS_DEV, 128).astype(F32) * cols[0]
+            for k in range(1, NY):
+                mixed += y_in[k, s, :, :, ln].reshape(NC * ROWS_DEV, 128).astype(F32) * cols[k]
+            mix[s, :, :, ln] = mixed.astype(BF16).reshape(NC, ROWS_DEV, 128)
+        for dc in range(NC):
+            if (dz, dc) != (0, 0):
+                send(("rz", (-dz) % NZ, dc), mix.at[s, (c + dc) % NC],
+                     out_ref.at[z, c], dev(dz=dz, dc=dc))
+
+    for dz in (4, 3, 5, 2, 6, 1, 7, 0):
+        mixing(SLOT[dz])
     last = pltpu.make_async_copy(mix.at[0, c], out_ref.at[z, c], loc_sem)
     last.start()
     last.wait()
@@ -432,10 +424,9 @@
             pltpu.VMEM((NZ, 16, 128), F32),
             pltpu.VMEM((8, 128), F32),
             pltpu.VMEM((8, 128), F32),
+            pltpu.VMEM((NY, 8, 128), F32),
             pltpu.VMEM((NY, NZ, NC, ROWS_DEV, VP), BF16),
-            pltpu.VMEM((2, 4, NC, ROWS_DEV, VP), BF16),
-            pltpu.VMEM((2, 4, NC, ROWS_DEV, VP), BF16),
-            pltpu.VMEM((2, 4, NC, ROWS_DEV, VP), BF16),
+            pltpu.VMEM((NY, NZ, NC, ROWS_DEV, VP), BF16),
             pltpu.VMEM((NZ, NC, ROWS_DEV, VP), BF16),
             pltpu.SemaphoreType.DMA,
             pltpu.SemaphoreType.DMA,

time: 91.9 us -> 87 us (0.947)
  Pallas kernels: 91.7 us -> 86.8 us
    pallas_call x1, Pallas kernels: 89.4 us -> 84.5 us  [per_device(): pl.pallas_call(body, out_shape=jax.ShapeDtypeStruct((NZ, NC, ROWS_DEV, VP...]
where the time goes in v3:
time: 87 us; the launch traced here: 86.8 us
  Pallas kernels  86.8 us (100%)
    pallas_call x1, Pallas kernels, per_device(): pl.pallas_call(body, out_shape=jax.ShapeDtypeStruct((NZ, NC, ROWS_DEV, VP...  84.5 us
    pallas_call x1, Pallas kernels, per_device(): pl.pallas_call(spread, out_shape=jax.ShapeDtypeStruct((ROWS_DEV, NZ * NC...  2.35 us

profile of v3, /device:TPU:1, one launch (start us, length us, event | category | flops | bytes accessed | tf_op | source)
XLA Modules:
  0.0 86.8 jit_solution(3479654265649882563)
XLA Ops:
  0.0 84.5 %shard_map.55.mix_ref = bf16[8,2,16,1024]{3,2,1,0:T(8,128)(2,1)} custom-call(bf16[16,4096]{1,0:T(8,128)(2,1)} %h_ref.1, f32[4,4096]{1,0:T(4,128)} %g_ref.1, s32[2,16]{1,0:T(2,128)} %bitcast.6, s32[2,16]{1,0:T(2,128)} %bitcast.7, bf16[1002,4096]{1,0:T(8,128)(2,1)} %bitcast.5), custom_call_target="tpu_custom_call" | custom-call | tf_op jit(solution)/shard_map/pallas_call | solution.py:407
  84.5 2.3 %shard_map.56 = f32[16,16032]{1,0:T(8,128)} custom-call(bf16[8,2,16,1024]{3,2,1,0:T(8,128)(2,1)} %shard_map.55.mix_ref), custom_call_target="tpu_custom_call" | custom-call | tf_op jit(solution)/shard_map/pallas_call | solution.py:439

commit v4 on v3

--- a/solution.py
+++ b/solution.py
@@ -80,7 +80,7 @@
     w_copy.start()
 
     peers = [dev(dy=k) for k in range(1, NY)]
-    peers += [dev(dz=1), dev(dz=-1), dev(dx=1), dev(dx=-1), dev(dc=1)]
+    peers += [dev(dz=1), dev(dz=-1), dev(dx=1), dev(dx=2), dev(dx=-1), dev(dc=1)]
     barrier = pltpu.get_barrier_semaphore()
     for peer in peers:
         pl.semaphore_signal(barrier, inc=1, device_id=peer, device_id_type=MESH)
@@ -205,6 +205,7 @@
             arrive(("y", k), gat.at[0, x, c, (y - k) % NY])
         a_along_z(0, k, 1)
         a_along_z(0, k, -1)
+    send(("bx", 2), part_b(0, 0), part_b(0, 0), dev(dx=2))
     send(("bx", 3), part_b(0, 0), part_b(0, 0), dev(dx=1))
     send(("bx", 1), part_b(0, 0), part_b(0, 0), dev(dx=-1))
     a_along_x(0)
@@ -214,8 +215,6 @@
 
     for dx in (3, 1, 2):
         arrive(("bx", dx), part_b(0, dx))
-        if dx == 3:
-            send(("bx", 2), part_b(0, 3), part_b(0, 3), dev(dx=1))
         b_along_z(0, dx, 1)
         b_along_z(0, dx, -1)
 
@@ -261,6 +260,13 @@
             if dz:
                 to_sibling(dz, 0)
             finish_x(dz)
+
+    def shares_out():
+        for dz in range(NZ):
+            for dc in range(NC):
+                if (dz, dc) != (0, 0):
+                    send(("sz", (-dz) % NZ, dc), sh_all.at[0, c], sh_all.at[(-dz) % NZ, c],
+                         dev(dz=dz, dc=dc))
 
     a_round(1)
     opposite(0)
@@ -281,9 +287,9 @@
     b_all(3)
     logits(0, 1)
     finish(2)
+    stats(0)
     opposite(4)
     b_all(4)
-    stats(0)
     from_sibling(1)
     from_sibling(6)
     logits(1, 0)
@@ -298,11 +304,7 @@
     stats(2)
     from_sibling(3)
     from_sibling(4)
-    for dz in range(NZ):
-        for dc in range(NC):
-            if (dz, dc) != (0, 0):
-                send(("sz", (-dz) % NZ, dc), sh_all.at[0, c], sh_all.at[(-dz) % NZ, c],
-                     dev(dz=dz, dc=dc))
+    shares_out()
     logits(3, 0)
     logits(3, 1)
     stats(3)

time: 87 us -> 83.2 us (0.956)
  Pallas kernels: 86.8 us -> 83.1 us
    pallas_call x1, Pallas kernels: 84.5 us -> 80.7 us  [per_device(): pl.pallas_call(body, out_shape=jax.ShapeDtypeStruct((NZ, NC, ROWS_DEV, VP...]
where the time goes in v4:
time: 83.2 us; the launch traced here: 83.1 us
  Pallas kernels  83.1 us (100%)
    pallas_call x1, Pallas kernels, per_device(): pl.pallas_call(body, out_shape=jax.ShapeDtypeStruct((NZ, NC, ROWS_DEV, VP...  80.7 us
    pallas_call x1, Pallas kernels, per_device(): pl.pallas_call(spread, out_shape=jax.ShapeDtypeStruct((ROWS_DEV, NZ * NC...  2.35 us

profile of v4, /device:TPU:1, one launch (start us, length us, event | category | flops | bytes accessed | tf_op | source)
XLA Modules:
  0.0 83.1 jit_solution(1627270711713945973)
XLA Ops:
  0.0 80.7 %shard_map.55.mix_ref = bf16[8,2,16,1024]{3,2,1,0:T(8,128)(2,1)} custom-call(bf16[16,4096]{1,0:T(8,128)(2,1)} %h_ref.1, f32[4,4096]{1,0:T(4,128)} %g_ref.1, s32[2,16]{1,0:T(2,128)} %bitcast.6, s32[2,16]{1,0:T(2,128)} %bitcast.7, bf16[1002,4096]{1,0:T(8,128)(2,1)} %bitcast.5), custom_call_target="tpu_custom_call" | custom-call | tf_op jit(solution)/shard_map/pallas_call | solution.py:409
  80.7 2.3 %shard_map.56 = f32[16,16032]{1,0:T(8,128)} custom-call(bf16[8,2,16,1024]{3,2,1,0:T(8,128)(2,1)} %shard_map.55.mix_ref), custom_call_target="tpu_custom_call" | custom-call | tf_op jit(solution)/shard_map/pallas_call | solution.py:441

commit v5 on v4

--- a/solution.py
+++ b/solution.py
@@ -160,7 +160,7 @@
 
     def logits(g, n):
         rows = 2 * 128
-        lo, hi = ((0, 512), (512, VD))[n]
+        lo, hi = ((0, 512), (512, VD), (0, VD))[n]
         acc = jnp.zeros((rows, hi - lo), F32)
         for xi in range(NX):
             lhs = gat[2 * g:2 * g + 2, xi].reshape(rows, FQ)
@@ -168,9 +168,9 @@
                 lhs, wt[lo:hi, xi * FQ:(xi + 1) * FQ],
                 (((1,), (1,)), ((), ())), preferred_element_type=F32)
         acc = acc * LOG2E
-        if n == 1:
+        if hi == VD:
             acc = jnp.concatenate([acc, jnp.full((rows, VP - VD), FAR, F32)], axis=1)
-        lg[g * rows:(g + 1) * rows, lo:lo + 512] = acc
+        lg[g * rows:(g + 1) * rows, lo:lo + acc.shape[1]] = acc
 
     def stats(g):
         rows = 2 * 128
@@ -289,24 +289,22 @@
     finish(2)
     stats(0)
     opposite(4)
-    b_all(4)
     from_sibling(1)
     from_sibling(6)
     logits(1, 0)
+    b_all(4)
     finish(3)
     finish(4)
     logits(1, 1)
     stats(1)
     from_sibling(2)
     from_sibling(5)
-    logits(2, 0)
-    logits(2, 1)
+    logits(2, 2)
     stats(2)
     from_sibling(3)
     from_sibling(4)
     shares_out()
-    logits(3, 0)
-    logits(3, 1)
+    logits(3, 2)
     stats(3)
 
     def merge(parts):

time: 83.2 us -> 83 us (level)
  no operation moved by 1% of the time
where the time goes in v5:
time: 83 us; the launch traced here: 82.8 us
  Pallas kernels  82.8 us (100%)
    pallas_call x1, Pallas kernels, per_device(): pl.pallas_call(body, out_shape=jax.ShapeDtypeStruct((NZ, NC, ROWS_DEV, VP...  80.5 us
    pallas_call x1, Pallas kernels, per_device(): pl.pallas_call(spread, out_shape=jax.ShapeDtypeStruct((ROWS_DEV, NZ * NC...  2.35 us

profile of v5, /device:TPU:1, one launch (start us, length us, event | category | flops | bytes accessed | tf_op | source)
XLA Modules:
  0.0 82.8 jit_solution(6984593553515211731)
XLA Ops:
  0.0 80.5 %shard_map.55.mix_ref = bf16[8,2,16,1024]{3,2,1,0:T(8,128)(2,1)} custom-call(bf16[16,4096]{1,0:T(8,128)(2,1)} %h_ref.1, f32[4,4096]{1,0:T(4,128)} %g_ref.1, s32[2,16]{1,0:T(2,128)} %bitcast.6, s32[2,16]{1,0:T(2,128)} %bitcast.7, bf16[1002,4096]{1,0:T(8,128)(2,1)} %bitcast.5), custom_call_target="tpu_custom_call" | custom-call | tf_op jit(solution)/shard_map/pallas_call | solution.py:407
  80.5 2.3 %shard_map.56 = f32[16,16032]{1,0:T(8,128)} custom-call(bf16[8,2,16,1024]{3,2,1,0:T(8,128)(2,1)} %shard_map.55.mix_ref), custom_call_target="tpu_custom_call" | custom-call | tf_op jit(solution)/shard_map/pallas_call | solution.py:439
